TPU v7x, 32 devices: a whole 2x2x4 slice. The times are simulated.
32 devices in a mesh: stream: 2 (over y), ta: 4 (over x, core), gz: 4 (over z).
Axes of the slice: x: 2, y: 2, z: 4, core: 2. Of those that a mesh axis runs over, the one named last changes fastest.
Arguments:
- links: float32 [4, 3, 3, 2, 32, 16, 128], P(None, None, None, None, ('stream', 'ta'), 'gz'), parts along dimension 4, may hold values from -2.1 to 2.1
- force_in: float32 [4, 3, 3, 2, 32, 16, 128], P(None, None, None, None, ('stream', 'ta'), 'gz'), parts along dimension 4, may hold values from -6 to 6
Outputs:
- force_out: float32 [4, 3, 3, 2, 32, 16, 128], P(None, None, None, None, ('stream', 'ta'), 'gz'), parts along dimension 4
There are 2 independent parts, one for each index of `stream`. A program takes and returns all parts, laid end to end along the dimension named above; each array names one. Nothing has to cross between parts.
All inputs are finite; a program needn't handle non-finite values.
Results may differ from a plain program's by a relative error of at most 0.0003.
Values sent between devices are 32-bit elements; how exact they have to be, the bound alone decides.
A program may use at most 128 MiB of HBM per device.

v0:
```python
import jax
import jax.numpy as jnp
from jax import lax
from jax.sharding import PartitionSpec as P

NX = 16
ORDER = 6


rho_value = 0.1


def extended(block, sides, width):
    for axis, dim in sides:
        count = lax.axis_size(axis)
        forward = [(i, i + 1) for i in range(count - 1)]
        forward.append((count - 1, 0))
        backward = [(target, source) for source, target in forward]
        low = lax.ppermute(
            lax.slice_in_dim(block, block.shape[dim] - width, None, axis=dim), axis, forward
        )
        high = lax.ppermute(lax.slice_in_dim(block, 0, width, axis=dim), axis, backward)
        block = jnp.concatenate([low, block, high], axis=dim)
    return block


def from_behind(value, axis, steps):
    count = lax.axis_size(axis)
    pairs = [(source, (source + steps) % count) for source in range(count)]
    return lax.ppermute(value, axis, pairs)


def product(left, right):
    left_real, left_imag = left
    right_real, right_imag = right
    real_part = jnp.sum(
        left_real[:, :, None] * right_real[None] - left_imag[:, :, None] * right_imag[None], axis=1
    )
    imag_part = jnp.sum(
        left_real[:, :, None] * right_imag[None] + left_imag[:, :, None] * right_real[None], axis=1
    )
    return (real_part, imag_part)


def dagger(matrix):
    return (jnp.swapaxes(matrix[0], 0, 1), -jnp.swapaxes(matrix[1], 0, 1))


def plus(first, second):
    return (first[0] + second[0], first[1] + second[1])


def scaled(first, factor):
    return (first[0] * factor, first[1] * factor)


def offset_of(direction, orient):
    return tuple((orient if position == direction else 0 for position in range(4)))


def joined(first, second):
    return tuple((left_part + right_part for left_part, right_part in zip(first, second)))


def make_locator(depth_rows, plane_sites):
    lanes = lax.broadcasted_iota(jnp.int32, (1, 1, 1, plane_sites), 3) % NX

    def move_one(field, offset):
        rows_step = offset[0] * depth_rows + offset[1]
        part = field
        if rows_step != 0:
            part = jnp.roll(part, -rows_step, axis=2)
        if offset[2] != 0:
            part = jnp.roll(part, -offset[2] * NX, axis=3)
        if offset[3] == 1:
            part = jnp.where(
                lanes == NX - 1, jnp.roll(part, NX - 1, axis=3), jnp.roll(part, -1, axis=3)
            )
        elif offset[3] == -1:
            part = jnp.where(
                lanes == 0, jnp.roll(part, -(NX - 1), axis=3), jnp.roll(part, 1, axis=3)
            )
        return part

    def locate(pair, offset):
        return (move_one(pair[0], offset), move_one(pair[1], offset))

    return locate


def fat_link(pair, direction, locate):
    anchor = (0, 0, 0, 0)
    field_real, field_imag = pair

    def pick(which):
        return (field_real[which], field_imag[which])

    center = locate(pick(direction), anchor)
    ahead = offset_of(direction, 1)
    staple_sum = (jnp.zeros_like(center[0]), jnp.zeros_like(center[1]))
    for other in range(4):
        if other == direction:
            continue
        beside = offset_of(other, 1)
        behind = offset_of(other, -1)
        upper_staple = product(
            product(locate(pick(other), anchor), locate(pick(direction), beside)),
            dagger(locate(pick(other), ahead)),
        )
        lower_staple = product(
            product(dagger(locate(pick(other), behind)), locate(pick(direction), behind)),
            locate(pick(other), joined(ahead, behind)),
        )
        staple_sum = plus(plus(staple_sum, upper_staple), lower_staple)
    omega_field = product(scaled(staple_sum, rho_value), dagger(center))
    omega_dag = dagger(omega_field)
    skew_part = (0.5 * (omega_field[0] - omega_dag[0]), 0.5 * (omega_field[1] - omega_dag[1]))
    unit_three = jnp.eye(3, dtype=jnp.float32).reshape((3, 3, 1, 1))
    trace_real = skew_part[0][0, 0] + skew_part[0][1, 1] + skew_part[0][2, 2]
    trace_imag = skew_part[1][0, 0] + skew_part[1][1, 1] + skew_part[1][2, 2]
    generator = (
        skew_part[0] - unit_three * trace_real[None, None] / 3.0,
        skew_part[1] - unit_three * trace_imag[None, None] / 3.0,
    )
    exponent = (unit_three + generator[0] / ORDER, generator[1] / ORDER)
    for degree in range(ORDER - 1, 0, -1):
        step_term = product(generator, exponent)
        exponent = (unit_three + step_term[0] / degree, step_term[1] / degree)
    return product(exponent, center)


def flat_parts(field):
    shape = field.shape
    merged = field.reshape(shape[:4] + (shape[4] * shape[5], shape[6]))
    return (merged[:, :, :, 0], merged[:, :, :, 1])


def pulled_total(padded, cotangent):
    depth_rows = padded.shape[5]
    plane_sites = padded.shape[6]
    locate = make_locator(depth_rows, plane_sites)
    links_real, links_imag = flat_parts(padded)
    force_real, force_imag = flat_parts(cotangent)
    total_real = jnp.zeros_like(links_real)
    total_imag = jnp.zeros_like(links_imag)
    for direction in range(4):
        pull_back = jax.vjp(
            lambda whole_real, whole_imag: fat_link((whole_real, whole_imag), direction, locate),
            links_real,
            links_imag,
        )[1]
        grad_real, grad_imag = pull_back((force_real[direction], force_imag[direction]))
        total_real = total_real + grad_real
        total_imag = total_imag + grad_imag
    return jnp.stack([total_real, total_imag], axis=3).reshape(padded.shape)


def per_device(links, force_in):
    rows_time = links.shape[4]
    rows_depth = links.shape[5]
    padded = extended(links, (("ta", 4), ("gz", 5)), 1)
    cotangent = jnp.pad(force_in, ((0, 0), (0, 0), (0, 0), (0, 0), (1, 1), (1, 1), (0, 0)))
    total = pulled_total(padded, cotangent)
    for orient, source, target in ((1, rows_time + 1, 1), (-1, 0, rows_time)):
        slab = lax.slice_in_dim(total, source, source + 1, axis=4)
        arrived = from_behind(slab, "ta", orient)
        total = total.at[:, :, :, :, target : target + 1].add(arrived)
    total = total[:, :, :, :, 1 : rows_time + 1]
    for orient, source, target in ((1, rows_depth + 1, 1), (-1, 0, rows_depth)):
        slab = lax.slice_in_dim(total, source, source + 1, axis=5)
        arrived = from_behind(slab, "gz", orient)
        total = total.at[:, :, :, :, :, target : target + 1].add(arrived)
    return total[:, :, :, :, :, 1 : rows_depth + 1]


def solution(mesh):
    placed = (
        P(None, None, None, None, ("stream", "ta"), "gz", None),
        P(None, None, None, None, ("stream", "ta"), "gz", None),
    )
    return jax.shard_map(
        per_device,
        mesh=mesh,
        in_specs=placed,
        out_specs=P(None, None, None, None, ("stream", "ta"), "gz", None),
        check_vma=False,
    )
```

profile of v0, /device:TPU:0, one launch (start us, length us, event | category | flops | bytes accessed | tf_op | source)
XLA Modules:
  0.0 289.8 jit_solution(7374795612737140785)
XLA Ops:
  0.0 1.1 fusion.264
  1.7 2.0 collective-permute-start.1
  4.4 1.0 fusion.261
  7.9 2.4 collective-permute-start.2
  10.3 2.6 collective-permute-start.3
  13.7 4.9 %collective-permute-done.2 = f32[4,3,3,2,6,1,128]{6,0,5,4,3,2,1:T(4,128)S(1)} collective-permute-done((f32[4,3,3,2,6,1,128]{6,0,5,4,3,2,1:T(4,128)S(1)}, f32[4,3,3,2,6,1,128]{6,0,5,4,3,2,1:T(4,128)S(1)}, u32[]{:S(2)}, u32[]{:S(2)}) %collective-permute-start.2) | collective-permute-done | bytes 221216 | tf_op jit(solution)/shard_map/ppermute | solution.py:19
  18.6 4.3 %collective-permute-done.3 = f32[4,3,3,2,6,1,128]{6,0,5,4,3,2,1:T(4,128)S(1)} collective-permute-done((f32[4,3,3,2,6,1,128]{6,0,5,4,3,2,1:T(4,128)S(1)}, f32[4,3,3,2,6,1,128]{6,0,5,4,3,2,1:T(4,128)S(1)}, u32[]{:S(2)}, u32[]{:S(2)}) %collective-permute-start.3) | collective-permute-done | bytes 221216 | tf_op jit(solution)/shard_map/ppermute | solution.py:22
  45.8 1.2 subtract_reduce_fusion.45
  49.9 1.7 multiply_reduce_fusion.386
  64.6 1.2 multiply_reduce_fusion.274
  65.9 1.4 multiply_reduce_fusion.378
  68.6 1.4 multiply_reduce_fusion.490
  71.3 1.3 multiply_reduce_fusion.481
  72.8 1.2 multiply_reduce_fusion.475
  74.0 1.4 multiply_reduce_fusion.369
  75.4 1.1 multiply_reduce_fusion.363
  76.6 1.2 multiply_reduce_fusion.469
  77.8 1.2 multiply_reduce_fusion.357
  79.0 5.3 %multiply_reduce_fusion.613 = (f32[36,128]{1,0:T(8,128)}, f32[36,128]{1,0:T(8,128)}, f32[36,128]{1,0:T(8,128)S(1)}, f32[36,128]{1,0:T(8,128)S(1)}, f32[3,3,36,12...) fusion(f32[3,3]{1,0:T(4,128)S(1)} %fusion.200, ...), kind=kLoop, calls=%fused_computation.1453 | loop fusion | flops 2469888 | bytes 8699940 | tf_op jit(solution)/shard_map/transpose(jvp())/reduce_sum | solution.py:123
  84.4 1.2 multiply_reduce_fusion.273
  86.7 2.3 multiply_reduce_fusion.324
  89.0 6.6 %multiply_reduce_fusion.334 = (f32[3,3,36,128]{3,2,1,0:T(8,128)}, f32[3,3,36,128]{3,2,1,0:T(8,128)}, f32[3,3,36,128]{3,2,1,0:T(8,128)}, f32[3,3,36,128]{3,2,1,0:...) fusion(f32[3,3,36,128]{3,2,1,0:T(8,128)} %copy-done.7, ...), kind=kLoop, calls=%fused_computation.448 | loop fusion | flops 6676992 | bytes 8460288 | tf_op jit(solution)/shard_map/transpose(jvp())/reduce_sum | solution.py:37
  95.6 1.1 add_any.3300
  103.3 1.2 multiply_reduce_fusion.385
  105.4 2.2 multiply_reduce_fusion.436
  107.7 4.6 %multiply_reduce_fusion.446 = (f32[3,3,36,128]{3,2,1,0:T(8,128)}, f32[3,3,36,128]{3,2,1,0:T(8,128)}, f32[3,3,36,128]{3,2,1,0:T(8,128)}, f32[3,3,36,128]{3,2,1,0:...) fusion(f32[3,3,36,128]{3,2,1,0:T(8,128)S(1)} %get-tuple-element, ...), kind=kLoop, calls=%fused_computation.596 | loop fusion | flops 6676992 | bytes 8460288 | tf_op jit(solution)/shard_map/transpose(jvp())/reduce_sum | solution.py:37
  112.3 1.1 add_any.3252
  114.1 1.1 add_any.2853
  120.7 2.5 multiply_reduce_fusion.498
  128.7 1.4 multiply_reduce_fusion.497
  131.0 1.9 multiply_reduce_fusion.528
  133.0 1.7 multiply_reduce_fusion.558
  147.1 1.3 multiply_reduce_fusion.551
  152.8 3.4 %multiply_reduce_fusion.542 = (f32[3,3,36,128]{3,2,1,0:T(8,128)}, f32[3,3,36,128]{3,2,1,0:T(8,128)}, f32[3,3,36,128]{3,2,1,0:T(8,128)}, f32[3,3,36,128]{3,2,1,0:...) fusion(f32[3,3,36,128]{3,2,1,0:T(8,128)S(1)} %get-tuple-element, ...), kind=kLoop, calls=%fused_computation.728 | loop fusion | flops 5598720 | bytes 7630848 | tf_op jit(solution)/shard_map/transpose(jvp())/reduce_sum | solution.py:37
  159.2 1.2 multiply_reduce_fusion.161
  161.2 1.8 multiply_reduce_fusion.222
  165.5 1.2 multiply_reduce_fusion.166
  171.8 1.3 multiply_reduce_fusion.512
  185.9 1.3 multiply_reduce_fusion.400
  222.2 1.4 multiply_reduce_fusion.532
  226.7 2.4 multiply_reduce_fusion.522
  230.9 2.0 multiply_reduce_fusion.502
  247.3 1.8 fusion.19
  262.9 1.8 fusion.38
  265.4 5.0 %collective-permute-done.4 = f32[4,3,3,2,1,6,128]{6,0,5,4,2,1,3:T(4,128)S(1)} collective-permute-done((f32[4,3,3,2,1,6,128]{6,0,5,4,2,1,3:T(4,128)S(1)}, f32[4,3,3,2,1,6,128]{6,0,5,4,2,1,3:T(4,128)S(1)}, u32[]{:S(2)}, u32[]{:S(2)}) %collective-permute-start.4) | collective-permute-done | bytes 221216 | tf_op jit(solution)/shard_map/ppermute | solution.py:30
  270.6 3.4 %collective-permute-done.5 = f32[4,3,3,2,1,6,128]{6,0,5,4,2,1,3:T(4,128)S(1)} collective-permute-done((f32[4,3,3,2,1,6,128]{6,0,5,4,2,1,3:T(4,128)S(1)}, f32[4,3,3,2,1,6,128]{6,0,5,4,2,1,3:T(4,128)S(1)}, u32[]{:S(2)}, u32[]{:S(2)}) %collective-permute-start.5) | collective-permute-done | bytes 221216 | tf_op jit(solution)/shard_map/ppermute | solution.py:30
  274.9 7.4 %collective-permute-done.6 = f32[4,3,3,2,4,1,128]{6,0,5,4,2,1,3:T(4,128)S(1)} collective-permute-done((f32[4,3,3,2,4,1,128]{6,0,5,4,2,1,3:T(4,128)S(1)}, f32[4,3,3,2,4,1,128]{6,0,5,4,2,1,3:T(4,128)S(1)}, u32[]{:S(2)}, u32[]{:S(2)}) %collective-permute-start.6) | collective-permute-done | bytes 147488 | tf_op jit(solution)/shard_map/ppermute | solution.py:30
  282.5 6.0 %collective-permute-done.7 = f32[4,3,3,2,4,1,128]{6,0,5,4,2,1,3:T(4,128)S(1)} collective-permute-done((f32[4,3,3,2,4,1,128]{6,0,5,4,2,1,3:T(4,128)S(1)}, f32[4,3,3,2,4,1,128]{6,0,5,4,2,1,3:T(4,128)S(1)}, u32[]{:S(2)}, u32[]{:S(2)}) %collective-permute-start.7) | collective-permute-done | bytes 147488 | tf_op jit(solution)/shard_map/ppermute | solution.py:30
  (1660 shorter events, 172.5 us)
Async XLA Ops:
  0.0 3.7 %copy-start.237 = (f32[4,3,3,2,4,4,128]{6,5,4,3,2,1,0:T(4,128)S(1)}, f32[4,3,3,2,4,4,128]{6,5,4,3,2,1,0:T(4,128)}, u32[]{:S(2)}) copy-start(f32[4,3,3,2,4,4,128]{6,5,4,3,2,1,0:T(4,128)} %param.11) | copy-start | bytes 1769476
  1.1 5.8 %collective-permute-start = (f32[4,3,3,2,1,4,128]{6,0,5,4,3,2,1:T(4,128)S(1)}, f32[4,3,3,2,1,4,128]{6,0,5,4,3,2,1:T(4,128)S(1)}, u32[]{:S(2)}, u32[]{:S(2)}) collective-permute-start(f32[4,3,3,2,1,4,128]{6,0,5,4,3,2,1:T(4,128)S(1)} %copy.2587), channel_id=1, source_target_pairs={{0,4},{4,8},{8,12},{12,0},{1,5},{5,9},{9,13},{13,1},{2,6},{6,10},{... | collective-permute-start | bytes 442376 | tf_op jit(solution)/shard_map/ppermute | solution.py:19
  1.7 6.1 %collective-permute-start.1 = (f32[4,3,3,2,1,4,128]{6,0,5,4,3,2,1:T(4,128)S(1)}, f32[4,3,3,2,1,4,128]{6,0,5,4,3,2,1:T(4,128)S(1)}, u32[]{:S(2)}, u32[]{:S(2)}) collective-permute-start(f32[4,3,3,2,1,4,128]{6,0,5,4,3,2,1:T(4,128)S(1)} %copy.2588), channel_id=1, source_target_pairs={{4,0},{8,4},{12,8},{0,12},{5,1},{9,5},{13,9},{1,13},{6,2},{10,6},{... | collective-permute-start | bytes 442376 | tf_op jit(solution)/shard_map/ppermute | solution.py:22
  6.9 34.7 %copy-start.294 = (pred[128]{0:T(512)(128)(4,1)}, pred[128]{0:T(512)(128)(4,1)S(1)}, u32[]{:S(2)}) copy-start(pred[128]{0:T(512)(128)(4,1)S(1)} %get-tuple-element.1330) | copy-start | bytes 388
  7.0 38.3 %copy-start.322 = (pred[128]{0:T(512)(128)(4,1)}, pred[128]{0:T(512)(128)(4,1)S(1)}, u32[]{:S(2)}) copy-start(pred[128]{0:T(512)(128)(4,1)S(1)} %get-tuple-element.1331) | copy-start | bytes 388
  7.9 10.7 %collective-permute-start.2 = (f32[4,3,3,2,6,1,128]{6,0,5,4,3,2,1:T(4,128)S(1)}, f32[4,3,3,2,6,1,128]{6,0,5,4,3,2,1:T(4,128)S(1)}, u32[]{:S(2)}, u32[]{:S(2)}) collective-permute-start(f32[4,3,3,2,6,1,128]{6,0,5,4,3,2,1:T(4,128)S(1)} %get-tuple-element.995), channel_id=1, source_target_pairs={{0,1},{1,2},{2,3},{3,0},{4,5},{5,6},{6,7},{7,4},{8,9},{9,10},{10,1... | collective-permute-start | bytes 663560 | tf_op jit(solution)/shard_map/ppermute | solution.py:19
  10.3 12.7 %collective-permute-start.3 = (f32[4,3,3,2,6,1,128]{6,0,5,4,3,2,1:T(4,128)S(1)}, f32[4,3,3,2,6,1,128]{6,0,5,4,3,2,1:T(4,128)S(1)}, u32[]{:S(2)}, u32[]{:S(2)}) collective-permute-start(f32[4,3,3,2,6,1,128]{6,0,5,4,3,2,1:T(4,128)S(1)} %get-tuple-element.996), channel_id=1, source_target_pairs={{1,0},{2,1},{3,2},{0,3},{5,4},{6,5},{7,6},{4,7},{9,8},{10,9},{11,1... | collective-permute-start | bytes 663560 | tf_op jit(solution)/shard_map/ppermute | solution.py:22
  24.3 29.5 %copy-start.292 = (f32[3,3,1,128]{3,2,0,1:T(1,128)}, f32[3,3,1,128]{3,2,0,1:T(1,128)S(1)}, u32[]{:S(2)}) copy-start(f32[3,3,1,128]{3,2,0,1:T(1,128)S(1)} %get-tuple-element.1093) | copy-start | bytes 13828
  24.3 12.8 %copy-start.260 = (f32[3,3,5,128]{3,2,0,1:T(8,128)}, f32[3,3,5,128]{3,2,0,1:T(8,128)S(1)}, u32[]{:S(2)}) copy-start(f32[3,3,5,128]{3,2,0,1:T(8,128)S(1)} %slice.1718) | copy-start | bytes 69124
  24.4 22.8 %copy-start.266 = (f32[3,3,6,128]{3,2,0,1:T(8,128)}, f32[3,3,6,128]{3,2,0,1:T(8,128)S(1)}, u32[]{:S(2)}) copy-start(f32[3,3,6,128]{3,2,0,1:T(8,128)S(1)} %get-tuple-element.1119) | copy-start | bytes 82948
  24.4 12.8 %copy-start.15 = (f32[3,3,31,128]{3,2,0,1:T(8,128)}, f32[3,3,31,128]{3,2,0,1:T(8,128)S(1)}, u32[]{:S(2)}) copy-start(f32[3,3,31,128]{3,2,0,1:T(8,128)S(1)} %slice.1719) | copy-start | bytes 428548
  25.2 26.6 %copy-start.258 = (f32[3,3,5,128]{3,2,0,1:T(8,128)}, f32[3,3,5,128]{3,2,0,1:T(8,128)S(1)}, u32[]{:S(2)}) copy-start(f32[3,3,5,128]{3,2,0,1:T(8,128)S(1)} %slice.1637) | copy-start | bytes 69124
  25.3 26.5 %copy-start.13 = (f32[3,3,31,128]{3,2,0,1:T(8,128)}, f32[3,3,31,128]{3,2,0,1:T(8,128)S(1)}, u32[]{:S(2)}) copy-start(f32[3,3,31,128]{3,2,0,1:T(8,128)S(1)} %slice.1636) | copy-start | bytes 428548
  26.6 20.6 %copy-start.11 = (f32[3,3,30,128]{3,2,0,1:T(8,128)}, f32[3,3,30,128]{3,2,0,1:T(8,128)S(1)}, u32[]{:S(2)}) copy-start(f32[3,3,30,128]{3,2,0,1:T(8,128)S(1)} %get-tuple-element.1121) | copy-start | bytes 414724
  30.3 17.4 %copy-start.264 = (f32[3,3,5,128]{3,2,0,1:T(8,128)}, f32[3,3,5,128]{3,2,0,1:T(8,128)S(1)}, u32[]{:S(2)}) copy-start(f32[3,3,5,128]{3,2,0,1:T(8,128)S(1)} %slice.1716) | copy-start | bytes 69124
  30.4 17.3 %copy-start.8 = (f32[3,3,31,128]{3,2,0,1:T(8,128)}, f32[3,3,31,128]{3,2,0,1:T(8,128)S(1)}, u32[]{:S(2)}) copy-start(f32[3,3,31,128]{3,2,0,1:T(8,128)S(1)} %slice.1717) | copy-start | bytes 428548
  33.7 20.5 %copy-start.262 = (f32[3,3,5,128]{3,2,0,1:T(8,128)}, f32[3,3,5,128]{3,2,0,1:T(8,128)S(1)}, u32[]{:S(2)}) copy-start(f32[3,3,5,128]{3,2,0,1:T(8,128)S(1)} %slice.1635) | copy-start | bytes 69124
  41.6 18.3 %copy-start = (f32[3,3,36,128]{3,2,0,1:T(8,128)}, f32[3,3,36,128]{3,2,0,1:T(8,128)S(1)}, u32[]{:S(2)}) copy-start(f32[3,3,36,128]{3,2,0,1:T(8,128)S(1)} %get-tuple-element.1315) | copy-start | bytes 497668
  51.6 8.9 %copy-start.2 = (f32[3,3,36,128]{3,2,1,0:T(8,128)}, f32[3,3,36,128]{3,2,1,0:T(8,128)S(1)}, u32[]{:S(2)}) copy-start(f32[3,3,36,128]{3,2,1,0:T(8,128)S(1)} %get-tuple-element.534) | copy-start | bytes 497668
  51.6 8.9 %copy-start.4 = (f32[3,3,36,128]{3,2,1,0:T(8,128)}, f32[3,3,36,128]{3,2,1,0:T(8,128)S(1)}, u32[]{:S(2)}) copy-start(f32[3,3,36,128]{3,2,1,0:T(8,128)S(1)} %get-tuple-element.535) | copy-start | bytes 497668
  85.7 3.3 %copy-start.6 = (f32[3,3,36,128]{3,2,1,0:T(8,128)}, f32[3,3,36,128]{3,2,1,0:T(8,128)S(1)}, u32[]{:S(2)}) copy-start(f32[3,3,36,128]{3,2,1,0:T(8,128)S(1)} %add_multiply_fusion.15) | copy-start | bytes 497668
  96.8 3.1 %copy-start.212 = (f32[3,3,36,128]{3,2,1,0:T(8,128)S(1)}, f32[3,3,36,128]{3,2,1,0:T(8,128)}, u32[]{:S(2)}) copy-start(f32[3,3,36,128]{3,2,1,0:T(8,128)} %get-tuple-element.594) | copy-start | bytes 497668
  96.8 3.1 %copy-start.219 = (f32[3,3,36,128]{3,2,1,0:T(8,128)S(1)}, f32[3,3,36,128]{3,2,1,0:T(8,128)}, u32[]{:S(2)}) copy-start(f32[3,3,36,128]{3,2,1,0:T(8,128)} %get-tuple-element.570) | copy-start | bytes 497668
  98.4 3.1 %copy-start.211 = (f32[3,3,36,128]{3,2,1,0:T(8,128)S(1)}, f32[3,3,36,128]{3,2,1,0:T(8,128)}, u32[]{:S(2)}) copy-start(f32[3,3,36,128]{3,2,1,0:T(8,128)} %get-tuple-element.595) | copy-start | bytes 497668
  98.4 3.1 %copy-start.218 = (f32[3,3,36,128]{3,2,1,0:T(8,128)S(1)}, f32[3,3,36,128]{3,2,1,0:T(8,128)}, u32[]{:S(2)}) copy-start(f32[3,3,36,128]{3,2,1,0:T(8,128)} %get-tuple-element.571) | copy-start | bytes 497668
  100.1 3.1 %copy-start.210 = (f32[3,3,36,128]{3,2,1,0:T(8,128)S(1)}, f32[3,3,36,128]{3,2,1,0:T(8,128)}, u32[]{:S(2)}) copy-start(f32[3,3,36,128]{3,2,1,0:T(8,128)} %get-tuple-element.934) | copy-start | bytes 497668
  100.1 3.1 %copy-start.291 = (f32[36,128]{1,0:T(8,128)S(1)}, f32[36,128]{1,0:T(8,128)}, u32[]{:S(2)}) copy-start(f32[36,128]{1,0:T(8,128)} %get-tuple-element.827) | copy-start | bytes 55300
  112.3 3.6 %copy-start.20 = (f32[3,3,36,128]{3,2,1,0:T(8,128)S(1)}, f32[3,3,36,128]{3,2,1,0:T(8,128)}, u32[]{:S(2)}) copy-start(f32[3,3,36,128]{3,2,1,0:T(8,128)} %get-tuple-element.472) | copy-start | bytes 497668
  112.3 3.6 %copy-start.44 = (f32[3,3,36,128]{3,2,1,0:T(8,128)S(1)}, f32[3,3,36,128]{3,2,1,0:T(8,128)}, u32[]{:S(2)}) copy-start(f32[3,3,36,128]{3,2,1,0:T(8,128)} %get-tuple-element.496) | copy-start | bytes 497668
  114.1 3.5 %copy-start.19 = (f32[3,3,36,128]{3,2,1,0:T(8,128)S(1)}, f32[3,3,36,128]{3,2,1,0:T(8,128)}, u32[]{:S(2)}) copy-start(f32[3,3,36,128]{3,2,1,0:T(8,128)} %get-tuple-element.473) | copy-start | bytes 497668
  114.1 3.5 %copy-start.42 = (f32[3,3,36,128]{3,2,1,0:T(8,128)S(1)}, f32[3,3,36,128]{3,2,1,0:T(8,128)}, u32[]{:S(2)}) copy-start(f32[3,3,36,128]{3,2,1,0:T(8,128)} %get-tuple-element.497) | copy-start | bytes 497668
  116.1 3.1 %copy-start.78 = (f32[3,3,36,128]{3,2,1,0:T(8,128)S(1)}, f32[3,3,36,128]{3,2,1,0:T(8,128)}, u32[]{:S(2)}) copy-start(f32[3,3,36,128]{3,2,1,0:T(8,128)} %get-tuple-element.163) | copy-start | bytes 497668
  134.7 3.4 %copy-start.45 = (f32[3,3,36,128]{3,2,1,0:T(8,128)S(1)}, f32[3,3,36,128]{3,2,1,0:T(8,128)}, u32[]{:S(2)}) copy-start(f32[3,3,36,128]{3,2,1,0:T(8,128)} %get-tuple-element.348) | copy-start | bytes 497668
  134.7 4.0 %copy-start.43 = (f32[3,3,36,128]{3,2,1,0:T(8,128)S(1)}, f32[3,3,36,128]{3,2,1,0:T(8,128)}, u32[]{:S(2)}) copy-start(f32[3,3,36,128]{3,2,1,0:T(8,128)} %get-tuple-element.349) | copy-start | bytes 497668
  136.4 3.0 %copy-start.41 = (f32[3,3,36,128]{3,2,1,0:T(8,128)S(1)}, f32[3,3,36,128]{3,2,1,0:T(8,128)}, u32[]{:S(2)}) copy-start(f32[3,3,36,128]{3,2,1,0:T(8,128)} %get-tuple-element.350) | copy-start | bytes 497668
  140.9 3.0 %copy-start.91 = (f32[3,3,36,128]{3,2,1,0:T(8,128)}, f32[3,3,36,128]{3,2,1,0:T(8,128)S(1)}, u32[]{:S(2)}) copy-start(f32[3,3,36,128]{3,2,1,0:T(8,128)S(1)} %fusion.165) | copy-start | bytes 497668
  142.4 3.1 %copy-start.295 = (pred[128]{0:T(512)(128)(4,1)S(1)}, pred[128]{0:T(512)(128)(4,1)}, u32[]{:S(2)}) copy-start(pred[128]{0:T(512)(128)(4,1)} %copy-done.294) | copy-start | bytes 388
  152.8 3.4 %copy-start.64 = (f32[3,3,36,128]{3,2,1,0:T(8,128)S(1)}, f32[3,3,36,128]{3,2,1,0:T(8,128)}, u32[]{:S(2)}) copy-start(f32[3,3,36,128]{3,2,1,0:T(8,128)} %get-tuple-element.716) | copy-start | bytes 497668
  152.8 3.5 %copy-start.46 = (f32[3,3,36,128]{3,2,1,0:T(8,128)S(1)}, f32[3,3,36,128]{3,2,1,0:T(8,128)}, u32[]{:S(2)}) copy-start(f32[3,3,36,128]{3,2,1,0:T(8,128)} %get-tuple-element.1352) | copy-start | bytes 497668
  152.8 3.5 %copy-start.47 = (f32[3,3,36,128]{3,2,1,0:T(8,128)S(1)}, f32[3,3,36,128]{3,2,1,0:T(8,128)}, u32[]{:S(2)}) copy-start(f32[3,3,36,128]{3,2,1,0:T(8,128)} %get-tuple-element.1225) | copy-start | bytes 497668
  181.6 3.3 %copy-start.170 = (f32[3,3,36,128]{3,2,1,0:T(8,128)S(1)}, f32[3,3,36,128]{3,2,1,0:T(8,128)}, u32[]{:S(2)}) copy-start(f32[3,3,36,128]{3,2,1,0:T(8,128)} %get-tuple-element.586) | copy-start | bytes 497668
  181.6 3.3 %copy-start.172 = (f32[3,3,36,128]{3,2,1,0:T(8,128)S(1)}, f32[3,3,36,128]{3,2,1,0:T(8,128)}, u32[]{:S(2)}) copy-start(f32[3,3,36,128]{3,2,1,0:T(8,128)} %get-tuple-element.560) | copy-start | bytes 497668
  182.2 2.7 copy-start.171
  199.4 3.2 %copy-start.27 = (f32[3,3,36,128]{3,2,1,0:T(8,128)S(1)}, f32[3,3,36,128]{3,2,1,0:T(8,128)}, u32[]{:S(2)}) copy-start(f32[3,3,36,128]{3,2,1,0:T(8,128)} %get-tuple-element.503) | copy-start | bytes 497668
  265.0 5.4 %collective-permute-start.4 = (f32[4,3,3,2,1,6,128]{6,0,5,4,2,1,3:T(4,128)S(1)}, f32[4,3,3,2,1,6,128]{6,0,5,4,2,1,3:T(4,128)S(1)}, u32[]{:S(2)}, u32[]{:S(2)}) collective-permute-start(f32[4,3,3,2,1,6,128]{6,0,5,4,2,1,3:T(4,128)S(1)} %fusion.42), channel_id=1, source_target_pairs={{0,4},{4,8},{8,12},{12,0},{1,5},{5,9},{9,13},{13,1},{2,6},{6,10},{... | collective-permute-start | bytes 663560 | tf_op jit(solution)/shard_map/ppermute | solution.py:30
  270.5 3.5 %collective-permute-start.5 = (f32[4,3,3,2,1,6,128]{6,0,5,4,2,1,3:T(4,128)S(1)}, f32[4,3,3,2,1,6,128]{6,0,5,4,2,1,3:T(4,128)S(1)}, u32[]{:S(2)}, u32[]{:S(2)}) collective-permute-start(f32[4,3,3,2,1,6,128]{6,0,5,4,2,1,3:T(4,128)S(1)} %slice.1907), channel_id=1, source_target_pairs={{0,12},{4,0},{8,4},{12,8},{1,13},{5,1},{9,5},{13,9},{2,14},{6,2},{... | collective-permute-start | bytes 663560 | tf_op jit(solution)/shard_map/ppermute | solution.py:30
  274.1 8.1 %collective-permute-start.6 = (f32[4,3,3,2,4,1,128]{6,0,5,4,2,1,3:T(4,128)S(1)}, f32[4,3,3,2,4,1,128]{6,0,5,4,2,1,3:T(4,128)S(1)}, u32[]{:S(2)}, u32[]{:S(2)}) collective-permute-start(f32[4,3,3,2,4,1,128]{6,0,5,4,2,1,3:T(4,128)S(1)} %slice.1910), channel_id=1, source_target_pairs={{0,1},{1,2},{2,3},{3,0},{4,5},{5,6},{6,7},{7,4},{8,9},{9,10},{10,1... | collective-permute-start | bytes 442376 | tf_op jit(solution)/shard_map/ppermute | solution.py:30
  282.4 6.1 %collective-permute-start.7 = (f32[4,3,3,2,4,1,128]{6,0,5,4,2,1,3:T(4,128)S(1)}, f32[4,3,3,2,4,1,128]{6,0,5,4,2,1,3:T(4,128)S(1)}, u32[]{:S(2)}, u32[]{:S(2)}) collective-permute-start(f32[4,3,3,2,4,1,128]{6,0,5,4,2,1,3:T(4,128)S(1)} %slice.1912), channel_id=1, source_target_pairs={{0,3},{1,0},{2,1},{3,2},{4,7},{5,4},{6,5},{7,6},{8,11},{9,8},{10,9... | collective-permute-start | bytes 442376 | tf_op jit(solution)/shard_map/ppermute | solution.py:30
  (313 other events, 393.0 us)
where the time goes:
time: 294 us; the launch traced here: 290 us
  other arithmetic  147 us (50%)
  local copies, waits for them, and re-layouts  95.8 us (33%)
  waiting for transfers between devices  31.1 us (11%)
  starting transfers between devices  8.36 us (3%)
  between operations  7.79 us (3%)
    reduce_sum x23, other arithmetic, product(): left_real[:, :, None] * right_real[None]  40.9 us
    split x127, local copies, waits for them, and re-layouts, move_one(): part = jnp.roll(part, -rows_step, axis=2)  40.3 us
    ppermute x4, waiting for transfers between devices, from_behind(): return lax.ppermute(value, axis, pairs)  21.8 us
    unnamed x657, local copies, waits for them, and re-layouts  21.3 us
    reduce_sum x28, other arithmetic, product(): left_imag[:, :, None] * right_real[None]  16 us
    reduce_sum x36, other arithmetic, product(): jnp.sum(left_real[:, :, None] * right_real[None] - left_imag[:, :, None]...  9.32 us
    add_any x12, other arithmetic, move_one(): part = jnp.roll(part, -offset[2] * NX, axis=3)  9.02 us
    broadcast_in_dim x127, other arithmetic, pick(): return (field_real[which], field_imag[which])  8.85 us
  transfers between devices with their start and end apart: 8, of which 7 were waited for; matrix products, arithmetic and copies ran while one was open for 2% of the time, Pallas kernels for 0%

commit v1 on v0

v1 whole, which is shorter than its diff:
```python
import jax
import jax.numpy as jnp
from jax import lax
from jax.experimental import pallas as pl
from jax.experimental.pallas import tpu as pltpu
from jax.sharding import PartitionSpec as P

NX = 16
RHO = 0.1
MESH = pl.DeviceIdType.MESH
ROWS = 16
COMPS = 18
FLAT = ROWS * COMPS
CHUNK = 48
FACE = FLAT // 4
T_FIELDS = (1, 2, 3)
Z_FIELDS = (0, 2, 3)


def comp_rows(i, j, part, start):
    return pl.ds(pl.multiple_of(((i * 3 + j) * 2 + part) * ROWS + start, 8), 8)


def read(ref, index, start):
    return [
        [
            (ref[index, comp_rows(i, j, 0, start), :], ref[index, comp_rows(i, j, 1, start), :])
            for j in range(3)
        ]
        for i in range(3)
    ]


def write(ref, index, start, i, j, value):
    ref[index, comp_rows(i, j, 0, start), :] = value[0]
    ref[index, comp_rows(i, j, 1, start), :] = value[1]


def add_to(ref, index, start, i, j, value):
    ref[index, comp_rows(i, j, 0, start), :] += value[0]
    ref[index, comp_rows(i, j, 1, start), :] += value[1]


def entry(terms, i, j):
    real = imag = None
    real_less = imag_less = None
    for left, left_dag, right, right_dag in terms:
        for k in range(3):
            a = left[k][i] if left_dag else left[i][k]
            b = right[j][k] if right_dag else right[k][j]
            rr, ii, ri, ir = a[0] * b[0], a[1] * b[1], a[0] * b[1], a[1] * b[0]
            real = rr if real is None else real + rr
            if left_dag == right_dag:
                real_less = ii if real_less is None else real_less + ii
            else:
                real = real + ii
            if right_dag:
                imag_less = ri if imag_less is None else imag_less + ri
            else:
                imag = ri if imag is None else imag + ri
            if left_dag:
                imag_less = ir if imag_less is None else imag_less + ir
            else:
                imag = ir if imag is None else imag + ir
    if real_less is not None:
        real = real - real_less
    if imag_less is not None:
        imag = imag - imag_less
    return real, imag


def products(terms, emit):
    for i in range(3):
        for j in range(3):
            emit(i, j, entry(terms, i, j))


def matrix(terms):
    return [[entry(terms, i, j) for j in range(3)] for i in range(3)]


def cmul(a, b):
    return a[0] * b[0] - a[1] * b[1], a[0] * b[1] + a[1] * b[0]


def plane_of(p):
    first, second = p // 3, p // 5
    return first + second, p + 1 - 2 * first - second


def forward_plane(p, start, u, sh, c, d, pr):
    mu, nu = plane_of(p)
    beside, above = mu * 4 + nu, nu * 4 + mu
    left = lambda: read(u, mu, start)
    up = lambda: read(u, nu, start)
    b_ = lambda: read(sh, beside, start)
    c_ = lambda: read(sh, above, start)
    products([(left(), False, b_(), False)], lambda i, j, v: write(pr, 2 * p, start, i, j, v))
    products([(up(), False, c_(), False)], lambda i, j, v: write(pr, 2 * p + 1, start, i, j, v))
    pp = lambda: read(pr, 2 * p, start)
    rr = lambda: read(pr, 2 * p + 1, start)
    products([(rr(), False, b_(), True)], lambda i, j, v: add_to(c, mu, start, i, j, v))
    products([(up(), True, pp(), False)], lambda i, j, v: write(d, above, start, i, j, v))
    products([(pp(), False, c_(), True)], lambda i, j, v: add_to(c, nu, start, i, j, v))
    products([(left(), True, rr(), False)], lambda i, j, v: write(d, beside, start, i, j, v))


def backward_plane(p, start, u, sh, g, shg, out, d, pr, tmp):
    mu, nu = plane_of(p)
    beside, above = mu * 4 + nu, nu * 4 + mu
    a_ = lambda: read(u, mu, start)
    d_ = lambda: read(u, nu, start)
    b_ = lambda: read(sh, beside, start)
    c_ = lambda: read(sh, above, start)
    ga = lambda: read(g, mu, start)
    gd = lambda: read(g, nu, start)
    gb = lambda: read(shg, beside, start)
    gc = lambda: read(shg, above, start)
    pp = lambda: read(pr, 2 * p, start)
    rr = lambda: read(pr, 2 * p + 1, start)
    gp = lambda: read(tmp, 0, 0)
    gr = lambda: read(tmp, 1, 0)
    products(
        [(d_(), False, gc(), False), (gd(), False, c_(), False)],
        lambda i, j, v: write(tmp, 0, 0, i, j, v),
    )
    products(
        [(ga(), False, b_(), False), (a_(), False, gb(), False)],
        lambda i, j, v: write(tmp, 1, 0, i, j, v),
    )
    products(
        [(gp(), False, b_(), True), (rr(), False, gb(), True)],
        lambda i, j, v: add_to(out, mu, start, i, j, v),
    )
    products(
        [(a_(), True, gp(), False), (ga(), True, rr(), False)],
        lambda i, j, v: write(d, beside, start, i, j, v),
    )
    products(
        [(d_(), True, gr(), False), (gd(), True, pp(), False)],
        lambda i, j, v: write(d, above, start, i, j, v),
    )
    products(
        [(gr(), False, c_(), True), (pp(), False, gc(), True)],
        lambda i, j, v: add_to(out, nu, start, i, j, v),
    )


def hermitian(m):
    out = [[None] * 3 for _ in range(3)]
    for i in range(3):
        out[i][i] = (m[i][i][0], None)
        for j in range(i + 1, 3):
            re = 0.5 * (m[i][j][0] + m[j][i][0])
            im = 0.5 * (m[i][j][1] - m[j][i][1])
            out[i][j] = (re, im)
            out[j][i] = (re, -im)
    return out


def traceless(m):
    third = (m[0][0][0] + m[1][1][0] + m[2][2][0]) * (1.0 / 3.0)
    return [
        [(m[i][j][0] - third, None) if i == j else m[i][j] for j in range(3)] for i in range(3)
    ]


def times_h(a, b):
    if a[1] is None and b[1] is None:
        return a[0] * b[0], None
    if a[1] is None:
        return a[0] * b[0], a[0] * b[1]
    if b[1] is None:
        return a[0] * b[0], a[1] * b[0]
    return cmul(a, b)


def plus_h(a, b):
    if a is None:
        return b
    im = b[1] if a[1] is None else (a[1] if b[1] is None else a[1] + b[1])
    return a[0] + b[0], im


def entry_h(left, right, i, j):
    total = None
    for k in range(3):
        total = plus_h(total, times_h(left[i][k], right[k][j]))
    return total


def exponent_step(mu, start, u, c, f, g, out):
    link = read(u, mu, start)
    force = read(f, mu, start)
    grad_e = matrix([(force, False, link, True)])
    stap = read(c, mu, start)
    omega = matrix([(stap, False, link, True)])
    turned = [[(RHO * omega[i][j][1], -RHO * omega[i][j][0]) for j in range(3)] for i in range(3)]
    q = traceless(hermitian(turned))
    q2 = [[None] * 3 for _ in range(3)]
    for i in range(3):
        for j in range(i, 3):
            if i == j:
                total = q[i][i][0] * q[i][i][0]
                for k in range(3):
                    if k != i:
                        total = total + q[i][k][0] * q[i][k][0] + q[i][k][1] * q[i][k][1]
                q2[i][i] = (total, None)
            else:
                q2[i][j] = entry_h(q, q, i, j)
                q2[j][i] = (q2[i][j][0], -q2[i][j][1])
    c1 = 0.5 * (q2[0][0][0] + q2[1][1][0] + q2[2][2][0])
    n01 = q[0][1][0] * q[0][1][0] + q[0][1][1] * q[0][1][1]
    n02 = q[0][2][0] * q[0][2][0] + q[0][2][1] * q[0][2][1]
    n12 = q[1][2][0] * q[1][2][0] + q[1][2][1] * q[1][2][1]
    loop = cmul(q[0][1], q[1][2])
    c0 = (
        q[0][0][0] * (q[1][1][0] * q[2][2][0] - n12)
        - q[1][1][0] * n02
        - q[2][2][0] * n01
        + 2.0 * (loop[0] * q[0][2][0] + loop[1] * q[0][2][1])
    )
    f0 = (1.0 - c0 * c0 * (1.0 / 720), c0 * (c1 * (1.0 / 120) - 1.0 / 6))
    f1 = (c0 * (1.0 / 24 - c1 * (1.0 / 360)), 1.0 + c1 * (c1 * (1.0 / 120) - 1.0 / 6))
    f2 = (-0.5 + c1 * (1.0 / 24 - c1 * (1.0 / 720)), c0 * (1.0 / 120))
    expo = [[None] * 3 for _ in range(3)]
    for i in range(3):
        for j in range(3):
            value = plus_h(times_h(f1, q[i][j]), times_h(f2, q2[i][j]))
            if i == j:
                value = (value[0] + f0[0], value[1] + f0[1])
            expo[i][j] = value
    direct = matrix([(expo, True, force, False)])
    t0 = (
        grad_e[0][0][0] + grad_e[1][1][0] + grad_e[2][2][0],
        -(grad_e[0][0][1] + grad_e[1][1][1] + grad_e[2][2][1]),
    )

    def paired(h):
        re = im = None
        for i in range(3):
            for j in range(3):
                ge = grad_e[i][j]
                value = times_h((ge[0], -ge[1]), h[i][j])
                re = value[0] if re is None else re + value[0]
                im = value[1] if im is None else im + value[1]
        return re, im

    t1, t2 = paired(q), paired(q2)
    slope = 1.0 / 24 - c1 * (1.0 / 360)
    b0 = (
        t0[0] * (c0 * (-1.0 / 360))
        - t0[1] * (c1 * (1.0 / 120) - 1.0 / 6)
        + t1[0] * slope
        - t2[1] * (1.0 / 120)
    )
    b1 = (
        t2[0] * slope
        - t0[1] * (c0 * (1.0 / 120))
        - t1[0] * (c0 * (1.0 / 360))
        - t1[1] * (c1 * (1.0 / 60) - 1.0 / 6)
    )
    f1c, f2c = (f1[0], -f1[1]), (f2[0], -f2[1])
    first = hermitian([[cmul(f1c, grad_e[i][j]) for j in range(3)] for i in range(3)])
    second = hermitian([[cmul(f2c, grad_e[i][j]) for j in range(3)] for i in range(3)])
    mixed = [[entry_h(q, second, i, j) for j in range(3)] for i in range(3)]
    gq = [[None] * 3 for _ in range(3)]
    for i in range(3):
        gq[i][i] = (
            first[i][i][0] + 2.0 * mixed[i][i][0] + b1 * q[i][i][0] + b0 * q2[i][i][0],
            None,
        )
        for j in range(i + 1, 3):
            re = first[i][j][0] + mixed[i][j][0] + mixed[j][i][0]
            im = first[i][j][1] + mixed[i][j][1] - mixed[j][i][1]
            re = re + b1 * q[i][j][0] + b0 * q2[i][j][0]
            im = im + b1 * q[i][j][1] + b0 * q2[i][j][1]
            gq[i][j] = (re, im)
            gq[j][i] = (re, -im)
    gq = traceless(gq)
    gq = [
        [(RHO * e[0], None if e[1] is None else RHO * e[1]) for e in row] for row in gq
    ]
    for i in range(3):
        for j in range(3):
            re, im = entry_h(gq, link, i, j)
            write(g, mu, start, i, j, (-im, re))
    for i in range(3):
        for j in range(3):
            re, im = entry_h(gq, stap, i, j)
            write(out, mu, start, i, j, (direct[i][j][0] + im, direct[i][j][1] - re))


def chunks(body):
    def step(k, carry):
        body(pl.ds(pl.multiple_of(k * CHUNK, 8), CHUNK))
        return carry

    lax.fori_loop(0, FLAT // CHUNK, step, 0)


def lanes_x():
    return lax.broadcasted_iota(jnp.int32, (CHUNK, 128), 1) % NX


def row_number():
    return lax.broadcasted_iota(jnp.int32, (CHUNK, 128), 0) % ROWS


def shift_down_local(src, dst):
    def body(rows):
        last_x = lanes_x() == NX - 1
        for f in range(4):
            v = src[f, rows, :]
            if f != 0:
                dst[f, rows, :] = pltpu.roll(v, CHUNK - 4, 0)
            if f != 1:
                dst[4 + f, rows, :] = pltpu.roll(v, CHUNK - 1, 0)
            if f != 2:
                dst[8 + f, rows, :] = pltpu.roll(v, 128 - NX, 1)
            if f != 3:
                dst[12 + f, rows, :] = jnp.where(
                    last_x, pltpu.roll(v, NX - 1, 1), pltpu.roll(v, 127, 1)
                )

    chunks(body)


def shift_up_local(src, dst):
    def body(rows):
        first_x = lanes_x() == 0
        row = row_number()
        first_t = row < 4
        first_z = row % 4 == 0
        for f in range(4):
            total = dst[f, rows, :]
            if f != 0:
                total = total + jnp.where(first_t, 0.0, pltpu.roll(src[f, rows, :], 4, 0))
            if f != 1:
                total = total + jnp.where(first_z, 0.0, pltpu.roll(src[4 + f, rows, :], 1, 0))
            if f != 2:
                total = total + pltpu.roll(src[8 + f, rows, :], NX, 1)
            if f != 3:
                v = src[12 + f, rows, :]
                total = total + jnp.where(
                    first_x, pltpu.roll(v, 128 - NX + 1, 1), pltpu.roll(v, 1, 1)
                )
            dst[f, rows, :] = total

    chunks(body)


def pack_t(src, indices, row, buf, phase):
    for n, index in enumerate(indices):
        for c in range(COMPS):
            buf[phase, n, pl.ds(c * 4, 4), :] = src[index, pl.ds(c * ROWS + row, 4), :]


def pack_z(src, indices, row, buf, phase):
    for n, index in enumerate(indices):
        for k in range(FACE // 8):
            buf[phase, n, pl.ds(k * 8, 8), :] = src[index, pl.ds(k * 32 + row, 8, stride=4), :]


def put_t(dst, indices, row, buf, phase, add):
    for n, index in enumerate(indices):
        for c in range(COMPS):
            v = buf[phase, n, pl.ds(c * 4, 4), :]
            where = pl.ds(c * ROWS + row, 4)
            if add:
                v = v + dst[index, where, :]
            dst[index, where, :] = v


def put_z(dst, indices, row, buf, phase, add):
    for n, index in enumerate(indices):
        for k in range(FACE // 8):
            v = buf[phase, n, pl.ds(k * 8, 8), :]
            where = pl.ds(k * 32 + row, 8, stride=4)
            if add:
                v = v + dst[index, where, :]
            dst[index, where, :] = v


def make_kernel(n_t, n_z):
    def kernel(
        u, f, out, c, g, sh, shg, d, pr, tmp, t_out, t_in, z_out, z_in,
        t_send, t_recv, z_send, z_recv,
    ):
        me_t, me_z = lax.axis_index("ta"), lax.axis_index("gz")
        t_up, t_down = lax.rem(me_t + 1, n_t), lax.rem(me_t + n_t - 1, n_t)
        z_up, z_down = lax.rem(me_z + 1, n_z), lax.rem(me_z + n_z - 1, n_z)
        barrier = pltpu.get_barrier_semaphore()
        for target in ({"ta": t_up}, {"ta": t_down}, {"gz": z_up}, {"gz": z_down}):
            pl.semaphore_signal(barrier, inc=1, device_id=target, device_id_type=MESH)

        def copies(phase, to_t, to_z):
            return (
                pltpu.make_async_remote_copy(
                    src_ref=t_out.at[phase], dst_ref=t_in.at[phase],
                    send_sem=t_send.at[phase], recv_sem=t_recv.at[phase],
                    device_id={"ta": to_t}, device_id_type=MESH,
                ),
                pltpu.make_async_remote_copy(
                    src_ref=z_out.at[phase], dst_ref=z_in.at[phase],
                    send_sem=z_send.at[phase], recv_sem=z_recv.at[phase],
                    device_id={"gz": to_z}, device_id_type=MESH,
                ),
            )

        t_pairs = T_FIELDS
        z_pairs = tuple(4 + n for n in Z_FIELDS)

        def send(phase, to_t, to_z):
            pair = copies(phase, to_t, to_z)
            for copy in pair:
                copy.start()
            return pair

        def planes(low, high, body):
            def step(n, carry):
                body(n // 2, (n % 2) * 8)
                return carry

            lax.fori_loop(2 * low, 2 * high, step, 0)

        pack_t(u, T_FIELDS, 0, t_out, 0)
        pack_z(u, Z_FIELDS, 0, z_out, 0)
        pl.semaphore_wait(barrier, 4)
        pair = send(0, t_down, z_down)
        c[...] = jnp.zeros_like(c)
        shift_down_local(u, sh)
        run_forward = lambda p, start: forward_plane(p, start, u, sh, c, d, pr)
        planes(5, 6, run_forward)
        pair[0].wait()
        put_t(sh, t_pairs, 12, t_in, 0, False)
        pair[1].wait()
        put_z(sh, z_pairs, 3, z_in, 0, False)
        planes(0, 5, run_forward)
        pack_t(d, t_pairs, 12, t_out, 1)
        pack_z(d, z_pairs, 3, z_out, 1)
        pair = send(1, t_up, z_up)
        shift_up_local(d, c)
        pair[0].wait()
        put_t(c, T_FIELDS, 0, t_in, 1, True)
        pair[1].wait()
        put_z(c, Z_FIELDS, 0, z_in, 1, True)

        def expo(n, carry):
            exponent_step(n // 2, (n % 2) * 8, u, c, f, g, out)
            return carry

        lax.fori_loop(0, 8, expo, 0)
        pack_t(g, T_FIELDS, 0, t_out, 2)
        pack_z(g, Z_FIELDS, 0, z_out, 2)
        pair = send(2, t_down, z_down)
        shift_down_local(g, shg)
        run_backward = lambda p, start: backward_plane(
            p, start, u, sh, g, shg, out, d, pr, tmp
        )
        planes(5, 6, run_backward)
        pair[0].wait()
        put_t(shg, t_pairs, 12, t_in, 2, False)
        pair[1].wait()
        put_z(shg, z_pairs, 3, z_in, 2, False)
        planes(0, 5, run_backward)
        pack_t(d, t_pairs, 12, t_out, 3)
        pack_z(d, z_pairs, 3, z_out, 3)
        pair = send(3, t_up, z_up)
        shift_up_local(d, out)
        pair[0].wait()
        put_t(out, T_FIELDS, 0, t_in, 3, True)
        pair[1].wait()
        put_z(out, Z_FIELDS, 0, z_in, 3, True)

    return kernel


def per_device(links, force_in):
    kernel = make_kernel(lax.axis_size("ta"), lax.axis_size("gz"))
    fields = lambda n: pltpu.VMEM((n, FLAT, 128), jnp.float32)
    faces = pltpu.VMEM((4, 3, FACE, 128), jnp.float32)
    out = pl.pallas_call(
        kernel,
        out_shape=jax.ShapeDtypeStruct((4, FLAT, 128), jnp.float32),
        in_specs=[pl.BlockSpec(memory_space=pltpu.VMEM)] * 2,
        out_specs=pl.BlockSpec(memory_space=pltpu.VMEM),
        scratch_shapes=[
            fields(4), fields(4), fields(16), fields(16), fields(16), fields(12),
            pltpu.VMEM((2, FLAT, 128), jnp.float32),
            faces, faces, faces, faces,
            pltpu.SemaphoreType.DMA((4,)), pltpu.SemaphoreType.DMA((4,)),
            pltpu.SemaphoreType.DMA((4,)), pltpu.SemaphoreType.DMA((4,)),
        ],
        compiler_params=pltpu.CompilerParams(
            collective_id=0, has_side_effects=True, vmem_limit_bytes=32 * 1024 * 1024
        ),
    )(links.reshape(4, FLAT, 128), force_in.reshape(4, FLAT, 128))
    return out.reshape(links.shape)


def solution(mesh):
    placed = P(None, None, None, None, ("stream", "ta"), "gz", None)
    return jax.shard_map(
        per_device,
        mesh=mesh,
        in_specs=(placed, placed),
        out_specs=placed,
        check_vma=False,
    )
```

time: 294 us -> 34.6 us (0.12); the launches traced: 290 us -> 34.4 us
  other arithmetic: 147 us -> 0 us
  local copies, waits for them, and re-layouts: 95.8 us -> 2.94 us
  Pallas kernels: 0 us -> 31.4 us
  waiting for transfers between devices: 31.1 us -> 0 us
  starting transfers between devices: 8.36 us -> 0 us
  between operations: 7.79 us -> 0.01 us
    reduce_sum x118 -> x0, other arithmetic: 83 us -> none  [the longest x23 40.9 us: product(): left_real[:, :, None] * right_real[None]]
    split x235 -> x0, local copies, waits for them, and re-layouts: 63.5 us -> none  [the longest x127 40.3 us: move_one(): part = jnp.roll(part, -rows_step, axis=2)]
    pallas_call x0 -> x1, Pallas kernels: none -> 31.4 us  [per_device(): pl.pallas_call(kernel, out_shape=jax.ShapeDtypeStruct((4, FLAT, 128), jnp...]
    ppermute x8 -> x0, waiting for transfers between devices: 31.1 us -> none  [the longest x4 21.8 us: from_behind(): return lax.ppermute(value, axis, pairs)]
    unnamed x657 -> x5, local copies, waits for them, and re-layouts: 21.3 us -> 2.94 us
    add_any x150 -> x0, other arithmetic: 18.3 us -> none  [the longest x12 9.02 us: move_one(): part = jnp.roll(part, -offset[2] * NX, axis=3)]
    slice x92 -> x0, local copies, waits for them, and re-layouts: 9.91 us -> none  [the longest x14 1.52 us: move_one(): part = jnp.roll(part, -offset[2] * NX, axis=3)]
    concatenate x90 -> x0, other arithmetic: 8.95 us -> none  [the longest x22 4.81 us: move_one(): part = jnp.roll(part, -offset[2] * NX, axis=3)]
  transfers between devices with their start and end apart: 8 -> 0, of which waited for: 7 -> 0; matrix products, arithmetic and copies ran while one was open for 2% -> 0% of each run, Pallas kernels for 0% -> 0%
where the time goes in v1:
time: 34.6 us; the launch traced here: 34.4 us
  Pallas kernels  31.4 us (91%)
  local copies, waits for them, and re-layouts  2.94 us (8%)
    pallas_call x1, Pallas kernels, per_device(): pl.pallas_call(kernel, out_shape=jax.ShapeDtypeStruct((4, FLAT, 128), jnp...  31.4 us
    unnamed x5, local copies, waits for them, and re-layouts  2.94 us

profile of v1, /device:TPU:0, one launch (start us, length us, event | category | flops | bytes accessed | tf_op | source)
XLA Modules:
  0.0 34.4 jit_solution(17207598057284034422)
XLA Ops:
  0.0 0.0 copy-start
  0.0 1.1 %copy-done = f32[4,3,3,2,4,4,128]{6,5,4,3,2,1,0:T(4,128)S(1)} copy-done((f32[4,3,3,2,4,4,128]{6,5,4,3,2,1,0:T(4,128)S(1)}, f32[4,3,3,2,4,4,128]{6,5,4,3,2,1,0:T(4,128)}, u32[]{:S(2)}) %copy-start) | copy-done | bytes 589848
  1.1 0.0 copy-start.1
  1.1 1.1 %copy-done.1 = f32[4,3,3,2,4,4,128]{6,5,4,3,2,1,0:T(4,128)S(1)} copy-done((f32[4,3,3,2,4,4,128]{6,5,4,3,2,1,0:T(4,128)S(1)}, f32[4,3,3,2,4,4,128]{6,5,4,3,2,1,0:T(4,128)}, u32[]{:S(2)}) %copy-start.1) | copy-done | bytes 589848
  2.1 31.4 %shard_map.28 = f32[4,288,128]{2,1,0:T(8,128)S(1)} custom-call(f32[4,288,128]{2,1,0:T(8,128)S(1)} %bitcast.4, f32[4,288,128]{2,1,0:T(8,128)S(1)} %bitcast.5), custom_call_target="tpu_custom_call" | custom-call | tf_op jit(solution)/shard_map/pallas_call | solution.py:483
  33.6 0.8 %copy.4 = f32[4,3,3,2,4,4,128]{6,5,4,3,2,1,0:T(4,128)} copy(f32[4,3,3,2,4,4,128]{6,5,4,3,2,1,0:T(4,128)S(1)} %bitcast.3) | data formatting | bytes 1179648
Async XLA Ops:
  0.0 1.1 %copy-start = (f32[4,3,3,2,4,4,128]{6,5,4,3,2,1,0:T(4,128)S(1)}, f32[4,3,3,2,4,4,128]{6,5,4,3,2,1,0:T(4,128)}, u32[]{:S(2)}) copy-start(f32[4,3,3,2,4,4,128]{6,5,4,3,2,1,0:T(4,128)} %param.2) | copy-start | bytes 1769476
  1.1 1.1 %copy-start.1 = (f32[4,3,3,2,4,4,128]{6,5,4,3,2,1,0:T(4,128)S(1)}, f32[4,3,3,2,4,4,128]{6,5,4,3,2,1,0:T(4,128)}, u32[]{:S(2)}) copy-start(f32[4,3,3,2,4,4,128]{6,5,4,3,2,1,0:T(4,128)} %param.3) | copy-start | bytes 1769476

commit v2 on v1

--- a/solution.py
+++ b/solution.py
@@ -13,8 +13,9 @@
 FLAT = ROWS * COMPS
 CHUNK = 48
 FACE = FLAT // 4
-T_FIELDS = (1, 2, 3)
-Z_FIELDS = (0, 2, 3)
+T_FIELDS = ((0, 1), (1, 2), (2, 3))
+Z_FIELDS = ((0, 0), (1, 2), (2, 3))
+ALL_FIELDS = ((0, 0), (1, 1), (2, 2), (3, 3))
 
 
 def comp_rows(i, j, part, start):
@@ -350,20 +351,20 @@
     chunks(body)
 
 
-def pack_t(src, indices, row, buf, phase):
-    for n, index in enumerate(indices):
+def pack_t(src, pairs, row, buf, phase):
+    for n, index in pairs:
         for c in range(COMPS):
             buf[phase, n, pl.ds(c * 4, 4), :] = src[index, pl.ds(c * ROWS + row, 4), :]
 
 
-def pack_z(src, indices, row, buf, phase):
-    for n, index in enumerate(indices):
+def pack_z(src, pairs, row, buf, phase):
+    for n, index in pairs:
         for k in range(FACE // 8):
             buf[phase, n, pl.ds(k * 8, 8), :] = src[index, pl.ds(k * 32 + row, 8, stride=4), :]
 
 
-def put_t(dst, indices, row, buf, phase, add):
-    for n, index in enumerate(indices):
+def put_t(dst, pairs, row, buf, phase, add):
+    for n, index in pairs:
         for c in range(COMPS):
             v = buf[phase, n, pl.ds(c * 4, 4), :]
             where = pl.ds(c * ROWS + row, 4)
@@ -372,8 +373,8 @@
             dst[index, where, :] = v
 
 
-def put_z(dst, indices, row, buf, phase, add):
-    for n, index in enumerate(indices):
+def put_z(dst, pairs, row, buf, phase, add):
+    for n, index in pairs:
         for k in range(FACE // 8):
             v = buf[phase, n, pl.ds(k * 8, 8), :]
             where = pl.ds(k * 32 + row, 8, stride=4)
@@ -382,40 +383,110 @@
             dst[index, where, :] = v
 
 
+def pack_corner(src, buf, phase):
+    for first, count in ((0, 8), (8, 8), (16, 2)):
+        buf[phase, pl.ds(first, count), :] = src[
+            1, pl.ds(first * ROWS + 3, count, stride=ROWS), :
+        ]
+
+
+def layer_beside(layer, phase, corner, dst, base):
+    v = layer[phase, 1]
+    lane = lax.broadcasted_iota(jnp.int32, v.shape, 1) % NX
+    dst[base] = pltpu.roll(v, FACE - 1, 0)
+    for first, count in ((0, 8), (8, 8), (16, 2)):
+        dst[base, pl.ds(first * 4 + 3, count, stride=4), :] = corner[phase, pl.ds(first, count), :]
+    dst[base + 1] = pltpu.roll(v, 128 - NX, 1)
+    dst[base + 2] = jnp.where(lane == NX - 1, pltpu.roll(v, NX - 1, 1), pltpu.roll(v, 127, 1))
+
+
+def read_layer(ref, *index):
+    def part(c):
+        return ref[(*index, pl.ds(c * 4, 4), slice(None))]
+
+    return [
+        [(part((i * 3 + j) * 2), part((i * 3 + j) * 2 + 1)) for j in range(3)] for i in range(3)
+    ]
+
+
+def layer_writer(ref, phase, n):
+    def emit(i, j, value):
+        c = (i * 3 + j) * 2
+        ref[phase, n, pl.ds(c * 4, 4), :] = value[0]
+        ref[phase, n, pl.ds(c * 4 + 4, 4), :] = value[1]
+
+    return emit
+
+
+def forward_layer(n, mu, layer, beside, result):
+    low = read_layer(layer, 0, 1)
+    pp = matrix([(read_layer(layer, 0, mu), False, read_layer(beside, n), False)])
+    products([(low, True, pp, False)], layer_writer(result, 0, n))
+
+
+def backward_layer(n, mu, layer, beside, result):
+    a, b = read_layer(layer, 0, mu), read_layer(beside, n)
+    ga, gb = read_layer(layer, 1, mu), read_layer(beside, 3 + n)
+    gr = matrix([(ga, False, b, False), (a, False, gb, False)])
+    pp = matrix([(a, False, b, False)])
+    products(
+        [(read_layer(layer, 0, 1), True, gr, False), (read_layer(layer, 1, 1), True, pp, False)],
+        layer_writer(result, 1, n),
+    )
+
+
 def make_kernel(n_t, n_z):
     def kernel(
-        u, f, out, c, g, sh, shg, d, pr, tmp, t_out, t_in, z_out, z_in,
-        t_send, t_recv, z_send, z_recv,
+        u_hbm, f_hbm, out, u, f, c, g, sh, shg, d, pr, tmp, t_out, t_in, z_out, z_in,
+        l_out, l_in, k_out, k_in, beside, local,
+        t_send, t_recv, z_send, z_recv, l_send, l_recv, k_send, k_recv, load_sem,
     ):
         me_t, me_z = lax.axis_index("ta"), lax.axis_index("gz")
         t_up, t_down = lax.rem(me_t + 1, n_t), lax.rem(me_t + n_t - 1, n_t)
         z_up, z_down = lax.rem(me_z + 1, n_z), lax.rem(me_z + n_z - 1, n_z)
+        loads = [pltpu.make_async_copy(u_hbm.at[k], u.at[k], load_sem.at[k]) for k in range(4)]
+        loads += [
+            pltpu.make_async_copy(f_hbm.at[k], f.at[k], load_sem.at[4 + k]) for k in range(4)
+        ]
+        for load in loads:
+            load.start()
         barrier = pltpu.get_barrier_semaphore()
-        for target in ({"ta": t_up}, {"ta": t_down}, {"gz": z_up}, {"gz": z_down}):
+        for target in (
+            {"ta": t_up}, {"ta": t_down}, {"gz": z_up}, {"gz": z_down},
+            {"ta": t_down, "gz": z_up}, {"ta": t_up, "gz": z_down},
+        ):
             pl.semaphore_signal(barrier, inc=1, device_id=target, device_id_type=MESH)
 
-        def copies(phase, to_t, to_z):
-            return (
-                pltpu.make_async_remote_copy(
-                    src_ref=t_out.at[phase], dst_ref=t_in.at[phase],
-                    send_sem=t_send.at[phase], recv_sem=t_recv.at[phase],
-                    device_id={"ta": to_t}, device_id_type=MESH,
-                ),
-                pltpu.make_async_remote_copy(
-                    src_ref=z_out.at[phase], dst_ref=z_in.at[phase],
-                    send_sem=z_send.at[phase], recv_sem=z_recv.at[phase],
-                    device_id={"gz": to_z}, device_id_type=MESH,
-                ),
+        t_pairs = T_FIELDS
+        z_pairs = tuple((n, 4 + index) for n, index in Z_FIELDS)
+        sent = []
+
+        def send(out_buf, in_buf, send_sem, recv_sem, slot, place, target):
+            copy = pltpu.make_async_remote_copy(
+                src_ref=out_buf.at[slot], dst_ref=in_buf.at[slot],
+                send_sem=send_sem.at[place], recv_sem=recv_sem.at[place],
+                device_id=target, device_id_type=MESH,
             )
-
-        t_pairs = T_FIELDS
-        z_pairs = tuple(4 + n for n in Z_FIELDS)
-
-        def send(phase, to_t, to_z):
-            pair = copies(phase, to_t, to_z)
-            for copy in pair:
-                copy.start()
-            return pair
+            copy.start()
+            sent.append(copy)
+            return copy
+
+        def send_t(phase, n, target):
+            return send(t_out, t_in, t_send, t_recv, (phase, n), phase * 3 + n, {"ta": target})
+
+        def send_z(phase, n):
+            return send(z_out, z_in, z_send, z_recv, (phase, n), phase * 3 + n, {"gz": z_down})
+
+        def send_layer(phase, n):
+            return send(l_out, l_in, l_send, l_recv, (phase, n), phase * 4 + n, {"gz": z_up})
+
+        def send_corner(phase):
+            target = {"ta": t_down, "gz": z_up}
+            return send(k_out, k_in, k_send, k_recv, phase, phase, target)
+
+        def finish(copies):
+            for copy in copies:
+                copy.wait_recv()
 
         def planes(low, high, body):
             def step(n, carry):
@@ -424,73 +495,112 @@
 
             lax.fori_loop(2 * low, 2 * high, step, 0)
 
+        for load in loads[:4]:
+            load.wait()
+        pack_z(u, Z_FIELDS, 0, z_out, 0)
+        pack_corner(u, k_out, 0)
+        pl.semaphore_wait(barrier, 6)
+        z_copies = [send_z(0, n) for n in range(3)]
+        k_copy = send_corner(0)
         pack_t(u, T_FIELDS, 0, t_out, 0)
-        pack_z(u, Z_FIELDS, 0, z_out, 0)
-        pl.semaphore_wait(barrier, 4)
-        pair = send(0, t_down, z_down)
+        t_copies = [send_t(0, n, t_down) for n in range(3)]
+        pack_z(u, ALL_FIELDS, 3, l_out, 0)
+        l_copies = [send_layer(0, n) for n in range(4)]
         c[...] = jnp.zeros_like(c)
         shift_down_local(u, sh)
         run_forward = lambda p, start: forward_plane(p, start, u, sh, c, d, pr)
         planes(5, 6, run_forward)
-        pair[0].wait()
+        finish(t_copies)
         put_t(sh, t_pairs, 12, t_in, 0, False)
-        pair[1].wait()
+        planes(1, 3, run_forward)
+        pack_t(d, t_pairs[1:], 12, t_out, 1)
+        t_copies = [send_t(1, n, t_up) for n in (1, 2)]
+        finish(z_copies)
         put_z(sh, z_pairs, 3, z_in, 0, False)
-        planes(0, 5, run_forward)
-        pack_t(d, t_pairs, 12, t_out, 1)
-        pack_z(d, z_pairs, 3, z_out, 1)
-        pair = send(1, t_up, z_up)
+        planes(0, 1, run_forward)
+        pack_t(d, t_pairs[:1], 12, t_out, 1)
+        t_copies.append(send_t(1, 0, t_up))
+        planes(3, 5, run_forward)
         shift_up_local(d, c)
-        pair[0].wait()
+        finish(l_copies)
+        k_copy.wait_recv()
+        layer_beside(l_in, 0, k_in, beside, 0)
+        for n, mu in Z_FIELDS:
+            forward_layer(n, mu, l_in, beside, local)
+        put_z(c, Z_FIELDS, 0, local, 0, True)
+        finish(t_copies)
         put_t(c, T_FIELDS, 0, t_in, 1, True)
-        pair[1].wait()
-        put_z(c, Z_FIELDS, 0, z_in, 1, True)
-
-        def expo(n, carry):
-            exponent_step(n // 2, (n % 2) * 8, u, c, f, g, out)
-            return carry
-
-        lax.fori_loop(0, 8, expo, 0)
-        pack_t(g, T_FIELDS, 0, t_out, 2)
-        pack_z(g, Z_FIELDS, 0, z_out, 2)
-        pair = send(2, t_down, z_down)
+
+        for load in loads[4:]:
+            load.wait()
+        z_copies, t_copies, l_copies = [], [], []
+        for mu in (1, 0, 2, 3):
+
+            def expo(n, carry, mu=mu):
+                exponent_step(mu, n * 8, u, c, f, g, out)
+                return carry
+
+            lax.fori_loop(0, 2, expo, 0)
+            pack_z(g, ALL_FIELDS[mu : mu + 1], 3, l_out, 1)
+            l_copies.append(send_layer(1, mu))
+            if mu == 1:
+                pack_corner(g, k_out, 1)
+                k_copy = send_corner(1)
+            else:
+                n = (0, 1, 1, 2)[mu]
+                pack_z(g, ((n, mu),), 0, z_out, 1)
+                z_copies.append(send_z(1, n))
+            if mu != 0:
+                pack_t(g, ((mu - 1, mu),), 0, t_out, 2)
+                t_copies.append(send_t(2, mu - 1, t_down))
         shift_down_local(g, shg)
         run_backward = lambda p, start: backward_plane(
             p, start, u, sh, g, shg, out, d, pr, tmp
         )
         planes(5, 6, run_backward)
-        pair[0].wait()
+        finish(t_copies)
         put_t(shg, t_pairs, 12, t_in, 2, False)
-        pair[1].wait()
-        put_z(shg, z_pairs, 3, z_in, 2, False)
-        planes(0, 5, run_backward)
-        pack_t(d, t_pairs, 12, t_out, 3)
-        pack_z(d, z_pairs, 3, z_out, 3)
-        pair = send(3, t_up, z_up)
+        planes(1, 3, run_backward)
+        pack_t(d, t_pairs[1:], 12, t_out, 3)
+        t_copies = [send_t(3, n, t_up) for n in (1, 2)]
+        finish(z_copies)
+        put_z(shg, z_pairs, 3, z_in, 1, False)
+        planes(0, 1, run_backward)
+        pack_t(d, t_pairs[:1], 12, t_out, 3)
+        t_copies.append(send_t(3, 0, t_up))
+        planes(3, 5, run_backward)
         shift_up_local(d, out)
-        pair[0].wait()
+        finish(l_copies)
+        k_copy.wait_recv()
+        layer_beside(l_in, 1, k_in, beside, 3)
+        for n, mu in Z_FIELDS:
+            backward_layer(n, mu, l_in, beside, local)
+        put_z(out, Z_FIELDS, 0, local, 1, True)
+        finish(t_copies)
         put_t(out, T_FIELDS, 0, t_in, 3, True)
-        pair[1].wait()
-        put_z(out, Z_FIELDS, 0, z_in, 3, True)
+        for copy in sent:
+            copy.wait_send()
 
     return kernel
 
 
 def per_device(links, force_in):
     kernel = make_kernel(lax.axis_size("ta"), lax.axis_size("gz"))
-    fields = lambda n: pltpu.VMEM((n, FLAT, 128), jnp.float32)
-    faces = pltpu.VMEM((4, 3, FACE, 128), jnp.float32)
+    held = lambda *extent: pltpu.VMEM((*extent, 128), jnp.float32)
+    fields = lambda n: held(n, FLAT)
+    sems = lambda n: pltpu.SemaphoreType.DMA((n,))
     out = pl.pallas_call(
         kernel,
         out_shape=jax.ShapeDtypeStruct((4, FLAT, 128), jnp.float32),
-        in_specs=[pl.BlockSpec(memory_space=pltpu.VMEM)] * 2,
+        in_specs=[pl.BlockSpec(memory_space=pltpu.HBM)] * 2,
         out_specs=pl.BlockSpec(memory_space=pltpu.VMEM),
         scratch_shapes=[
-            fields(4), fields(4), fields(16), fields(16), fields(16), fields(12),
-            pltpu.VMEM((2, FLAT, 128), jnp.float32),
-            faces, faces, faces, faces,
-            pltpu.SemaphoreType.DMA((4,)), pltpu.SemaphoreType.DMA((4,)),
-            pltpu.SemaphoreType.DMA((4,)), pltpu.SemaphoreType.DMA((4,)),
+            fields(4), fields(4),
+            fields(4), fields(4), fields(16), fields(16), fields(16), fields(12), fields(2),
+            held(4, 3, FACE), held(4, 3, FACE), held(2, 3, FACE), held(2, 3, FACE),
+            held(2, 4, FACE), held(2, 4, FACE), held(2, 24), held(2, 24),
+            held(6, FACE), held(2, 3, FACE),
+            sems(12), sems(12), sems(6), sems(6), sems(8), sems(8), sems(2), sems(2), sems(8),
         ],
         compiler_params=pltpu.CompilerParams(
             collective_id=0, has_side_effects=True, vmem_limit_bytes=32 * 1024 * 1024

time: 34.6 us -> 31 us (0.90)
  Pallas kernels: 31.4 us -> 27.8 us
    pallas_call x1, Pallas kernels: 31.4 us -> 27.8 us  [per_device(): pl.pallas_call(kernel, out_shape=jax.ShapeDtypeStruct((4, FLAT, 128), jnp...]
where the time goes in v2:
time: 31 us; the launch traced here: 30.8 us
  Pallas kernels  27.8 us (90%)
  local copies, waits for them, and re-layouts  2.94 us (9%)
    pallas_call x1, Pallas kernels, per_device(): pl.pallas_call(kernel, out_shape=jax.ShapeDtypeStruct((4, FLAT, 128), jnp...  27.8 us
    unnamed x5, local copies, waits for them, and re-layouts  2.94 us

profile of v2, /device:TPU:0, one launch (start us, length us, event | category | flops | bytes accessed | tf_op | source)
XLA Modules:
  0.0 30.8 jit_solution(1830828246795179965)
XLA Ops:
  0.0 0.0 copy-start
  0.0 1.1 %copy-done = f32[4,3,3,2,4,4,128]{6,5,4,3,2,1,0:T(4,128)S(1)} copy-done((f32[4,3,3,2,4,4,128]{6,5,4,3,2,1,0:T(4,128)S(1)}, f32[4,3,3,2,4,4,128]{6,5,4,3,2,1,0:T(4,128)}, u32[]{:S(2)}) %copy-start) | copy-done | bytes 589848
  1.1 0.0 copy-start.1
  1.1 1.1 %copy-done.1 = f32[4,3,3,2,4,4,128]{6,5,4,3,2,1,0:T(4,128)S(1)} copy-done((f32[4,3,3,2,4,4,128]{6,5,4,3,2,1,0:T(4,128)S(1)}, f32[4,3,3,2,4,4,128]{6,5,4,3,2,1,0:T(4,128)}, u32[]{:S(2)}) %copy-start.1) | copy-done | bytes 589848
  2.1 27.8 %shard_map.28 = f32[4,288,128]{2,1,0:T(8,128)S(1)} custom-call(f32[4,288,128]{2,1,0:T(8,128)S(1)} %bitcast.4, f32[4,288,128]{2,1,0:T(8,128)S(1)} %bitcast.5), custom_call_target="tpu_custom_call" | custom-call | tf_op jit(solution)/shard_map/pallas_call | solution.py:592
  30.0 0.8 %copy.4 = f32[4,3,3,2,4,4,128]{6,5,4,3,2,1,0:T(4,128)} copy(f32[4,3,3,2,4,4,128]{6,5,4,3,2,1,0:T(4,128)S(1)} %bitcast.3) | data formatting | bytes 1179648
Async XLA Ops:
  0.0 1.1 %copy-start = (f32[4,3,3,2,4,4,128]{6,5,4,3,2,1,0:T(4,128)S(1)}, f32[4,3,3,2,4,4,128]{6,5,4,3,2,1,0:T(4,128)}, u32[]{:S(2)}) copy-start(f32[4,3,3,2,4,4,128]{6,5,4,3,2,1,0:T(4,128)} %param.2) | copy-start | bytes 1769476
  1.1 1.1 %copy-start.1 = (f32[4,3,3,2,4,4,128]{6,5,4,3,2,1,0:T(4,128)S(1)}, f32[4,3,3,2,4,4,128]{6,5,4,3,2,1,0:T(4,128)}, u32[]{:S(2)}) copy-start(f32[4,3,3,2,4,4,128]{6,5,4,3,2,1,0:T(4,128)} %param.3) | copy-start | bytes 1769476
